TPU v7x, 128 devices: a whole 4x4x4 slice. The times are simulated.
128 devices in a mesh: gx: 8 (over z, core), gy: 16 (over y, x).
Axes of the slice: x: 4, y: 4, z: 4, core: 2. Of those that a mesh axis runs over, the one named last changes fastest.
Arguments:
- increment: bfloat16 [128, 256, 384], P('gx', 'gy'), may hold values from -6 to 6
- vertical: bfloat16 [384, 384], replicated, may hold values from -0.3125 to 0.3125
- col_reach: float32 [384], replicated
- stretch_x: float32 [128, 256], P('gx', 'gy')
- stretch_y: float32 [128, 256], P('gx', 'gy')
Outputs:
- covaried: float32 [128, 256, 384], P('gx', 'gy')
All inputs are finite; a program needn't handle non-finite values.
Results may differ from a plain program's by a relative error of at most 0.0003.
Values sent between devices are 32-bit elements; how exact they have to be, the bound alone decides.
A program may use at most 64 MiB of HBM per device.

v0:
```python
import functools
import math

import jax
import jax.numpy as jnp
from jax import lax
from jax.experimental import pallas as pl
from jax.experimental.pallas import tpu as pltpu
from jax.sharding import PartitionSpec as P

MESH = pl.DeviceIdType.MESH
B = 16
NX, NY, NZ = 8, 16, 4
C, W, CT = 384, 128, 3
OFFSETS_Y = sorted([(a, b) for a in range(4) for b in range(4) if a or b],
                   key=lambda o: -min(o[0], 4 - o[0]) - min(o[1], 4 - o[1]))
PAIRS = [(a, b) for a in range(4) for b in range(a, 4)]


def cascade(state, u, p, q):
    out = []
    for k in range(4):
        u = p * state[k] + q * u
        out.append(u)
    return out, u


def toeplitz(t, s, add):
    out = []
    for k in range(4):
        total = add[k]
        for m in range(k + 1):
            total = total + t[k - m] * s[m]
        out.append(total)
    return out


def reflect(g, s, add):
    out = []
    for a in range(4):
        total = add[a]
        for m in range(4):
            total = total + g[PAIRS.index((min(a, 3 - m), max(a, 3 - m)))] * s[m]
        out.append(total)
    return out


def transfer(rates, scale, reflecting):
    c, g = None, [None] * 10
    for rate in rates:
        p = jnp.exp(rate * scale)
        q = 1.0 - p
        if c is None:
            d = [jnp.ones_like(p), q]
            d.append(q * d[1])
            d.append(q * d[2])
        else:
            d = [c[0]]
            for k in range(1, 4):
                d.append(c[k] + q * d[k - 1])
        c = [p * x for x in d]
        if reflecting:
            e = [q * x for x in c]
            for n, (a, b) in enumerate(PAIRS):
                term = d[a] * e[b]
                g[n] = term if g[n] is None else g[n] + term
    return (c, g) if reflecting else c


def columns(tile):
    return [tile[:, i:i + 1] for i in range(B)]


def sweep(source, poles, mid, rows_of, first, second, sink=None):
    state = first
    for i in range(B):
        rows = pl.ds(i * B, B)
        p = poles[rows, :]
        state, w = cascade(state, source[rows_of(i), :], p, 1.0 - p)
        mid[rows, :] = w
    ahead, state = state, second
    for i in reversed(range(B)):
        rows = pl.ds(i * B, B)
        p = poles[rows, :]
        state, w = cascade(state, mid[rows, :], p, 1.0 - p)
        if sink is not None:
            sink(i, w)
    return ahead + state


def chain(got, coefs, reply):
    zero = [jnp.zeros((1, W), jnp.float32)] * 4

    def at(ref, j, k):
        return ref[j, k:k + 1, :]

    s, entered = zero, []
    for j in range(NY):
        entered.append(s)
        for k in range(4):
            reply[j, k:k + 1, :] = s[k]
        s = toeplitz([at(coefs, j, k) for k in range(4)], s, [at(got, j, k) for k in range(4)])
    b = zero
    for j in reversed(range(NY)):
        for k in range(4):
            reply[j, 4 + k:5 + k, :] = b[k]
        g = [at(coefs, j, 4 + n) for n in range(10)]
        add = reflect(g, entered[j], [at(got, j, 4 + k) for k in range(4)])
        b = toeplitz([at(coefs, j, k) for k in range(4)], b, add)


def kernel(inc_hbm, vert_hbm, reach_hbm, sx_hbm, sy_hbm, out,
           inc, vert, reach_line, sx, sy, load_sem, u, px, py, mid,
           ends_x, pair, own, chips, passing, to_z, from_z, back, entering, ys1, yr1, ys2, yr2,
           tgy, sxs, sxr, sys_, syr, pole_send, pole_recv, pair_send, pair_recv, z_send, z_recv,
           back_send, back_recv, y_send, y_recv):
    gx, gy = lax.axis_index("gx"), lax.axis_index("gy")
    z, core = gx // 2, lax.rem(gx, 2)
    other = (gx + 1 - 2 * core, gy)

    def peer_y(dy, dx):
        return lax.rem(gy // 4 + dy, 4) * 4 + lax.rem(gy + dx, 4)

    barrier = pltpu.get_barrier_semaphore()
    for r in range(1, NX):
        pl.semaphore_signal(barrier, inc=1, device_id=(lax.rem(gx + r, NX), gy), device_id_type=MESH)
    for offset in OFFSETS_Y:
        pl.semaphore_signal(barrier, inc=1, device_id=(gx, peer_y(*offset)), device_id_type=MESH)

    loads = [pltpu.make_async_copy(src, dst, load_sem.at[n]) for n, (src, dst) in enumerate(
        [(sx_hbm, sx), (reach_hbm, reach_line), (vert_hbm, vert), (inc_hbm, inc), (sy_hbm, sy)])]
    for load in loads:
        load.start()

    def remote(src, dst, sent, got, device):
        return pltpu.make_async_remote_copy(src, dst, sent, got, device_id=device, device_id_type=MESH)

    def start_y(src, dst, sent, got):
        for offset in OFFSETS_Y:
            peer = peer_y(*offset)
            remote(src.at[peer], dst.at[gy], sent, got, (gx, peer)).start()
        dst[gy] = src[gy]

    def wait_for(part, sem):
        pltpu.make_async_copy(part, part, sem).wait()

    def lanes(ct):
        return slice(ct * W, (ct + 1) * W)

    loads[0].wait()
    loads[1].wait()
    reach = reach_line[...].reshape(1, C)
    rate_x = -1.0 / sx[...].T
    inverse_x = 1.0 / (reach * float(NX * B))
    inverse_y = 1.0 / (reach * float(NY * B))
    for i in range(B):
        for ct in range(CT):
            px[ct, pl.ds(i * B, B), :] = jnp.exp(rate_x[:, i:i + 1] * inverse_x[:, lanes(ct)])
    loads[4].wait()
    rate_y = -1.0 / sy[...]
    for half in range(2):
        sxs[half, :, 0:B] = rate_x[8 * half:8 * half + 8]
        sys_.reshape(NY * 8, W)[pl.ds(64 * half, 8, stride=8), 0:B] = rate_y[8 * half:8 * half + 8]
    loads[2].wait()
    loads[3].wait()
    mixed = jnp.dot(inc[...], vert[...], preferred_element_type=jnp.float32)
    for ct in range(CT):
        u[ct] = mixed[:, lanes(ct)]

    pl.semaphore_wait(barrier, NX + NY - 2)
    remote(sxs.at[1 - core], sxr.at[gx], pole_send.at[0], pole_recv.at[0], other).start()
    for r in (2, 1, 3):
        for c in range(2):
            peer = 2 * lax.rem(z + r, NZ) + c
            remote(sxs.at[c], sxr.at[gx], pole_send.at[1], pole_recv.at[1], (peer, gy)).start()
    sxr[gx] = sxs[core]

    zeros = [jnp.zeros((B, W), jnp.float32)] * 4
    nothing = [jnp.zeros((8, W), jnp.float32)] * 4

    def along(i):
        return pl.ds(i * B, B)

    def across(i):
        return pl.ds(i, B, stride=B)

    for ct in range(CT):
        ends = sweep(u.at[ct], px.at[ct], mid.at[ct], along, zeros, zeros)
        for half in range(2):
            for k in range(8):
                ends_x[ct, half, k] = ends[k][8 * half:8 * half + 8]
        remote(ends_x.at[ct, 1 - core], pair.at[ct, core], pair_send.at[ct], pair_recv.at[ct], other).start()
        pair[ct, core] = ends_x[ct, core]

    def start_z(ct, r, kind):
        peer = lax.rem(z + r, NZ)
        return remote(to_z.at[ct, kind], from_z.at[ct, z, kind], z_send.at[ct, peer, kind],
                      z_recv.at[ct, z, kind], (2 * peer + core, gy))

    def blocks(ct):
        t0, t1 = [own[ct, k] for k in range(4)], [own[ct, 4 + k] for k in range(4)]
        g1 = [own[ct, 8 + n] for n in range(10)]
        return t0, t1, g1, [[pair[ct, b, k] for k in range(8)] for b in range(2)]

    wait_for(sxr.at[0], pole_recv.at[0])
    first, second = columns(sxr[2 * z]), columns(sxr[2 * z + 1])
    for ct in range(CT):
        scale = inverse_x[:, lanes(ct)]
        t, g = transfer(second, scale, True)
        for k, value in enumerate(transfer(first, scale, False) + t + g):
            own[ct, k] = value
    for ct in range(CT):
        wait_for(pair.at[ct, 0], pair_recv.at[ct])
        t0, t1, g1, (e0, e1) = blocks(ct)
        ahead = toeplitz(t1, e0[:4], e1[:4])
        behind = toeplitz(t0, reflect(g1, e0[:4], e1[4:]), e0[4:])
        for k in range(4):
            to_z[ct, 0, k] = ahead[k]
            to_z[ct, 1, k] = behind[k]
        for r in (2, 1, 3):
            pl.when(z < NZ - 1)(lambda ct=ct, r=r: start_z(ct, r, 0).start())
            pl.when(lax.rem(z + r, NZ) < z)(lambda ct=ct, r=r: start_z(ct, r, 1).start())

    start_y(sys_, syr, pole_send.at[2], pole_recv.at[2])
    wait_for(sxr.at[pl.ds(0, NX - 2)], pole_recv.at[1])
    for ct in range(CT):
        scale = inverse_x[:, lanes(ct)]

        def stretches(m):
            return columns(sxr[2 * m]) + columns(sxr[2 * m + 1])

        def left(m, _):
            for k, value in enumerate(transfer(stretches(m), scale, False)):
                chips[m, ct, k] = value
            return 0

        def right(m, _):
            t, g = transfer(stretches(m), scale, True)
            for k, value in enumerate(t + g):
                chips[m, ct, k] = value
            return 0

        lax.fori_loop(0, z, left, 0)
        lax.fori_loop(z + 1, NZ, right, 0)

        def chip(m):
            return [chips[m, ct, k] for k in range(4)]

        def came(m, kind):
            wait_for(from_z.at[ct, m, kind], z_recv.at[ct, m, kind])
            return [from_z[ct, m, kind, k] for k in range(4)]

        def ahead(m, s):
            return toeplitz(chip(m), s, came(m, 0))

        def onward(m, s):
            s = ahead(m, s)
            for k in range(4):
                passing[ct, m + 1, k] = s[k]
            return s

        def behind(i, b):
            m = NZ - 1 - i
            g = [chips[m, ct, 4 + n] for n in range(10)]
            return toeplitz(chip(m), b, reflect(g, [passing[ct, m, k] for k in range(4)], came(m, 1)))

        s0 = lax.fori_loop(0, z, ahead, nothing)
        t0, t1, g1, (e0, e1) = blocks(ct)
        s1 = toeplitz(t0, s0, e0[:4])
        s2 = toeplitz(t1, s1, e1[:4])
        for k in range(4):
            passing[ct, z + 1, k] = s2[k]
        lax.fori_loop(z + 1, NZ - 1, onward, s2)
        b1 = lax.fori_loop(0, NZ - 1 - z, behind, nothing)
        b0 = toeplitz(t1, b1, reflect(g1, s1, e1[4:]))
        for b, states in enumerate([s0 + b0, s1 + b1]):
            for k in range(8):
                back[ct, b, k] = states[k]
        remote(back.at[ct, 1 - core], entering.at[ct, core], back_send.at[ct], back_recv.at[ct], other).start()
        entering[ct, core] = back[ct, core]

    for i in range(B):
        for ct in range(CT):
            py[ct, pl.ds(i * B, B), :] = jnp.exp(rate_y[:, i:i + 1] * inverse_y[:, lanes(ct)])

    for ct in range(CT):
        wait_for(entering.at[ct, 0], back_recv.at[ct])
        states = [jnp.concatenate([entering[ct, half, k] for half in range(2)], axis=0) for k in range(8)]

        def keep(i, w):
            u[ct, along(i), :] = w

        sweep(u.at[ct], px.at[ct], mid.at[ct], along, states[:4], states[4:], keep)
        ends = sweep(u.at[ct], py.at[ct], mid.at[ct], across, zeros, zeros)
        flat = ys1.at[ct].reshape(NY * 8, W)
        for k in range(8):
            for l in range(2):
                flat[pl.ds(64 * l + k, 8, stride=8), :] = ends[k][8 * l:8 * l + 8]
        start_y(ys1.at[ct], yr1.at[ct], y_send.at[0, ct], y_recv.at[0, ct])

    wait_for(syr.at[pl.ds(0, NY - 1)], pole_recv.at[2])
    rates = columns(syr.reshape(NY * 8, W)[pl.ds(0, NY, stride=8), 0:B])
    for ct in range(CT):
        t, g = transfer(rates, inverse_y[:, lanes(ct)], True)
        flat = tgy.at[ct].reshape(NY * 16, W)
        for k, value in enumerate(t + g):
            for l in range(2):
                flat[pl.ds(128 * l + k, 8, stride=16), :] = value[8 * l:8 * l + 8]

    for ct in range(CT):
        wait_for(yr1.at[ct, pl.ds(0, NY - 1)], y_recv.at[0, ct])
        chain(yr1.at[ct], tgy.at[ct], ys2.at[ct])
        start_y(ys2.at[ct], yr2.at[ct], y_send.at[1, ct], y_recv.at[1, ct])

    amplitude = 10.0 * jnp.minimum(reach, 0.25) * math.sqrt(NX * B * NY * B)
    for ct in range(CT):
        wait_for(yr2.at[ct, pl.ds(0, NY - 1)], y_recv.at[1, ct])
        flat = yr2.at[ct].reshape(NY * 8, W)
        states = [flat[pl.ds(k, NY, stride=8), :] for k in range(8)]

        def finish(i, w):
            u[ct, across(i), :] = w * amplitude[:, lanes(ct)]

        sweep(u.at[ct], py.at[ct], mid.at[ct], across, states[:4], states[4:], finish)
        out[:, lanes(ct)] = u[ct]

    wait_for(sxr.at[0], pole_send.at[0])
    wait_for(sxr.at[pl.ds(0, NX - 2)], pole_send.at[1])
    wait_for(syr.at[pl.ds(0, NY - 1)], pole_send.at[2])
    for ct in range(CT):
        wait_for(pair.at[ct, 0], pair_send.at[ct])
        for r in range(1, NZ):
            pl.when(z < NZ - 1)(lambda ct=ct, r=r: start_z(ct, r, 0).wait_send())
            pl.when(lax.rem(z + r, NZ) < z)(lambda ct=ct, r=r: start_z(ct, r, 1).wait_send())
        wait_for(entering.at[ct, 0], back_send.at[ct])
        wait_for(ys1.at[ct, pl.ds(0, NY - 1)], y_send.at[0, ct])
        wait_for(ys2.at[ct, pl.ds(0, NY - 1)], y_send.at[1, ct])


def shards(increment, vertical, col_reach, stretch_x, stretch_y):
    f32 = jnp.float32
    field = pltpu.VMEM((CT, B * B, W), f32)

    def states(*lead):
        return pltpu.VMEM(lead + (8, W), f32)

    def dma(*shape):
        return pltpu.SemaphoreType.DMA(shape)

    two, lines = states(CT, 2, 8), states(CT, NY)
    operands = (increment.reshape(B * B, C), vertical, col_reach, stretch_x, stretch_y)
    result = pl.pallas_call(
        kernel,
        out_shape=jax.ShapeDtypeStruct((B * B, C), f32),
        in_specs=[pl.BlockSpec(memory_space=pltpu.HBM)] * 5,
        out_specs=pl.BlockSpec(memory_space=pltpu.VMEM),
        scratch_shapes=[
            pltpu.VMEM((B * B, C), jnp.bfloat16), pltpu.VMEM((C, C), jnp.bfloat16), pltpu.VMEM((C,), f32),
            pltpu.VMEM((B, B), f32), pltpu.VMEM((B, B), f32), dma(5),
            field, field, field, field,
            two, two, states(CT, 18), states(NZ, CT, 14), states(CT, NZ + 1, 4),
            states(CT, 2, 4), states(CT, NZ, 2, 4), two, two,
            lines, lines, lines, lines, pltpu.VMEM((CT, NY, 16, W), f32),
            states(2), states(NX), states(NY), states(NY),
            dma(3), dma(3), dma(CT), dma(CT), dma(CT, NZ, 2), dma(CT, NZ, 2),
            dma(CT), dma(CT), dma(2, CT), dma(2, CT),
        ],
        compiler_params=pltpu.CompilerParams(
            collective_id=0, has_side_effects=True, vmem_limit_bytes=32 * 2**20),
        name="covariance",
    )(*[pltpu.with_memory_space_constraint(x, pltpu.HBM) for x in operands])
    return result.reshape(B, B, C)


def solution(mesh):
    in_specs = (P("gx", "gy", None), P(), P(), P("gx", "gy"), P("gx", "gy"))
    out_specs = P("gx", "gy", None)
    return jax.shard_map(shards, mesh=mesh, in_specs=in_specs, out_specs=out_specs, check_vma=False)
```

profile of v0, /device:TPU:1, one launch (start us, length us, event | category | flops | bytes accessed | tf_op | source)
XLA Modules:
  0.0 27.7 jit_solution(6933461911995287511)
XLA Ops:
  0.0 27.0 %covariance.1 = f32[256,384]{1,0:T(8,128)S(1)} custom-call(bf16[256,384]{1,0:T(8,128)(2,1)} %bitcast.3, bf16[384,384]{1,0:T(8,128)(2,1)} %vert_hbm.1, f32[384]{0:T(512)} %reach_hbm.1, f32[16,16]{1,0:T(8,128)} %sx_hbm.1, f32[16,16]{1,0:T(8,128)} %sy_hbm.1), custom_call_target="tpu_custom_call" | custom-call | tf_op jit(solution)/shard_map/covariance/pallas_call | solution.py:352
  27.0 0.7 %copy.7 = f32[16,16,384]{2,1,0:T(8,128)} copy(f32[16,16,384]{2,1,0:T(8,128)S(1)} %bitcast.2) | data formatting | bytes 786432
where the time goes:
time: 27.9 us; the launch traced here: 27.7 us
  Pallas kernels  27 us (97%)
  local copies, waits for them, and re-layouts  0.75 us (3%)
    pallas_call x1, Pallas kernels, shards(): pl.pallas_call(kernel, out_shape=jax.ShapeDtypeStruct((B * B, C), f32), i...  27 us
    unnamed x1, local copies, waits for them, and re-layouts  0.75 us

commit v1 on v0

--- a/solution.py
+++ b/solution.py
@@ -112,11 +112,12 @@
 def kernel(inc_hbm, vert_hbm, reach_hbm, sx_hbm, sy_hbm, out,
            inc, vert, reach_line, sx, sy, load_sem, u, px, py, mid,
            ends_x, pair, own, chips, passing, to_z, from_z, back, entering, ys1, yr1, ys2, yr2,
-           tgy, sxs, sxr, sys_, syr, pole_send, pole_recv, pair_send, pair_recv, z_send, z_recv,
-           back_send, back_recv, y_send, y_recv):
+           tgy, sxs, sxr, sys_, syr, sent, z_sent, y_sent, beside_recv, chip_recv, lines_recv, pair_recv,
+           z_recv, back_recv, gather_recv, reply_recv):
     gx, gy = lax.axis_index("gx"), lax.axis_index("gy")
     z, core = gx // 2, lax.rem(gx, 2)
     other = (gx + 1 - 2 * core, gy)
+    owner = 2 * z + 1
 
     def peer_y(dy, dx):
         return lax.rem(gy // 4 + dy, 4) * 4 + lax.rem(gy + dx, 4)
@@ -125,7 +126,12 @@
     for r in range(1, NX):
         pl.semaphore_signal(barrier, inc=1, device_id=(lax.rem(gx + r, NX), gy), device_id_type=MESH)
     for offset in OFFSETS_Y:
-        pl.semaphore_signal(barrier, inc=1, device_id=(gx, peer_y(*offset)), device_id_type=MESH)
+        pl.semaphore_signal(barrier, inc=1, device_id=(owner, peer_y(*offset)), device_id_type=MESH)
+
+    @pl.when(core == 1)
+    def _():
+        for offset in OFFSETS_Y:
+            pl.semaphore_signal(barrier, inc=1, device_id=(owner - 1, peer_y(*offset)), device_id_type=MESH)
 
     loads = [pltpu.make_async_copy(src, dst, load_sem.at[n]) for n, (src, dst) in enumerate(
         [(sx_hbm, sx), (reach_hbm, reach_line), (vert_hbm, vert), (inc_hbm, inc), (sy_hbm, sy)])]
@@ -135,11 +141,18 @@
     def remote(src, dst, sent, got, device):
         return pltpu.make_async_remote_copy(src, dst, sent, got, device_id=device, device_id_type=MESH)
 
-    def start_y(src, dst, sent, got):
+    def to_owners(src, dst, got):
         for offset in OFFSETS_Y:
             peer = peer_y(*offset)
-            remote(src.at[peer], dst.at[gy], sent, got, (gx, peer)).start()
-        dst[gy] = src[gy]
+            remote(src.at[peer], dst.at[core, gy], y_sent.at[0], got, (owner, peer)).start()
+
+        @pl.when(core == 0)
+        def _():
+            remote(src.at[gy], dst.at[0, gy], y_sent.at[0], got, (owner, gy)).start()
+
+        @pl.when(core == 1)
+        def _():
+            dst[1, gy] = src[gy]
 
     def wait_for(part, sem):
         pltpu.make_async_copy(part, part, sem).wait()
@@ -167,14 +180,6 @@
     for ct in range(CT):
         u[ct] = mixed[:, lanes(ct)]
 
-    pl.semaphore_wait(barrier, NX + NY - 2)
-    remote(sxs.at[1 - core], sxr.at[gx], pole_send.at[0], pole_recv.at[0], other).start()
-    for r in (2, 1, 3):
-        for c in range(2):
-            peer = 2 * lax.rem(z + r, NZ) + c
-            remote(sxs.at[c], sxr.at[gx], pole_send.at[1], pole_recv.at[1], (peer, gy)).start()
-    sxr[gx] = sxs[core]
-
     zeros = [jnp.zeros((B, W), jnp.float32)] * 4
     nothing = [jnp.zeros((8, W), jnp.float32)] * 4
 
@@ -189,27 +194,36 @@
         for half in range(2):
             for k in range(8):
                 ends_x[ct, half, k] = ends[k][8 * half:8 * half + 8]
-        remote(ends_x.at[ct, 1 - core], pair.at[ct, core], pair_send.at[ct], pair_recv.at[ct], other).start()
+
+    pl.semaphore_wait(barrier, NX + NY - 2 + core * (NY - 1))
+    remote(sxs.at[1 - core], sxr.at[gx], sent.at[0], beside_recv.at[0], other).start()
+    for ct in range(CT):
+        remote(ends_x.at[ct, 1 - core], pair.at[ct, core], sent.at[0], pair_recv.at[ct], other).start()
+    for r in (2, 1, 3):
+        for c in range(2):
+            peer = 2 * lax.rem(z + r, NZ) + c
+            remote(sxs.at[c], sxr.at[gx], sent.at[0], chip_recv.at[z], (peer, gy)).start()
+    sxr[gx] = sxs[core]
+    for ct in range(CT):
         pair[ct, core] = ends_x[ct, core]
 
     def start_z(ct, r, kind):
         peer = lax.rem(z + r, NZ)
-        return remote(to_z.at[ct, kind], from_z.at[ct, z, kind], z_send.at[ct, peer, kind],
-                      z_recv.at[ct, z, kind], (2 * peer + core, gy))
+        return remote(to_z.at[ct, kind], from_z.at[ct, z, kind], z_sent.at[0], z_recv.at[ct],
+                      (2 * peer + core, gy))
 
     def blocks(ct):
         t0, t1 = [own[ct, k] for k in range(4)], [own[ct, 4 + k] for k in range(4)]
         g1 = [own[ct, 8 + n] for n in range(10)]
         return t0, t1, g1, [[pair[ct, b, k] for k in range(8)] for b in range(2)]
 
-    wait_for(sxr.at[0], pole_recv.at[0])
+    wait_for(sxr.at[0], beside_recv.at[0])
     first, second = columns(sxr[2 * z]), columns(sxr[2 * z + 1])
     for ct in range(CT):
         scale = inverse_x[:, lanes(ct)]
         t, g = transfer(second, scale, True)
         for k, value in enumerate(transfer(first, scale, False) + t + g):
             own[ct, k] = value
-    for ct in range(CT):
         wait_for(pair.at[ct, 0], pair_recv.at[ct])
         t0, t1, g1, (e0, e1) = blocks(ct)
         ahead = toeplitz(t1, e0[:4], e1[:4])
@@ -221,33 +235,39 @@
             pl.when(z < NZ - 1)(lambda ct=ct, r=r: start_z(ct, r, 0).start())
             pl.when(lax.rem(z + r, NZ) < z)(lambda ct=ct, r=r: start_z(ct, r, 1).start())
 
-    start_y(sys_, syr, pole_send.at[2], pole_recv.at[2])
-    wait_for(sxr.at[pl.ds(0, NX - 2)], pole_recv.at[1])
-    for ct in range(CT):
-        scale = inverse_x[:, lanes(ct)]
-
-        def stretches(m):
-            return columns(sxr[2 * m]) + columns(sxr[2 * m + 1])
-
-        def left(m, _):
-            for k, value in enumerate(transfer(stretches(m), scale, False)):
+    to_owners(sys_, syr, lines_recv.at[0])
+
+    def stretches(m):
+        wait_for(sxr.at[pl.ds(0, 2)], chip_recv.at[m])
+        return columns(sxr[2 * m]) + columns(sxr[2 * m + 1])
+
+    def left(m, _):
+        rates = stretches(m)
+        for ct in range(CT):
+            for k, value in enumerate(transfer(rates, inverse_x[:, lanes(ct)], False)):
                 chips[m, ct, k] = value
-            return 0
-
-        def right(m, _):
-            t, g = transfer(stretches(m), scale, True)
+        return 0
+
+    def right(m, _):
+        rates = stretches(m)
+        for ct in range(CT):
+            t, g = transfer(rates, inverse_x[:, lanes(ct)], True)
             for k, value in enumerate(t + g):
                 chips[m, ct, k] = value
-            return 0
-
-        lax.fori_loop(0, z, left, 0)
-        lax.fori_loop(z + 1, NZ, right, 0)
+        return 0
+
+    lax.fori_loop(0, z, left, 0)
+    lax.fori_loop(z + 1, NZ, right, 0)
+
+    for ct in range(CT):
+        for chip_z, messages in enumerate((5, 4, 3, 3)):
+            pl.when(z == chip_z)(lambda ct=ct, messages=messages: wait_for(
+                from_z.at[ct].reshape(2 * NZ, 4, 8, W).at[pl.ds(0, messages)], z_recv.at[ct]))
 
         def chip(m):
             return [chips[m, ct, k] for k in range(4)]
 
         def came(m, kind):
-            wait_for(from_z.at[ct, m, kind], z_recv.at[ct, m, kind])
             return [from_z[ct, m, kind, k] for k in range(4)]
 
         def ahead(m, s):
@@ -276,7 +296,7 @@
         for b, states in enumerate([s0 + b0, s1 + b1]):
             for k in range(8):
                 back[ct, b, k] = states[k]
-        remote(back.at[ct, 1 - core], entering.at[ct, core], back_send.at[ct], back_recv.at[ct], other).start()
+        remote(back.at[ct, 1 - core], entering.at[ct, core], sent.at[0], back_recv.at[ct], other).start()
         entering[ct, core] = back[ct, core]
 
     for i in range(B):
@@ -296,25 +316,36 @@
         for k in range(8):
             for l in range(2):
                 flat[pl.ds(64 * l + k, 8, stride=8), :] = ends[k][8 * l:8 * l + 8]
-        start_y(ys1.at[ct], yr1.at[ct], y_send.at[0, ct], y_recv.at[0, ct])
-
-    wait_for(syr.at[pl.ds(0, NY - 1)], pole_recv.at[2])
-    rates = columns(syr.reshape(NY * 8, W)[pl.ds(0, NY, stride=8), 0:B])
-    for ct in range(CT):
-        t, g = transfer(rates, inverse_y[:, lanes(ct)], True)
-        flat = tgy.at[ct].reshape(NY * 16, W)
-        for k, value in enumerate(t + g):
-            for l in range(2):
-                flat[pl.ds(128 * l + k, 8, stride=16), :] = value[8 * l:8 * l + 8]
-
-    for ct in range(CT):
-        wait_for(yr1.at[ct, pl.ds(0, NY - 1)], y_recv.at[0, ct])
-        chain(yr1.at[ct], tgy.at[ct], ys2.at[ct])
-        start_y(ys2.at[ct], yr2.at[ct], y_send.at[1, ct], y_recv.at[1, ct])
+        to_owners(ys1.at[ct], yr1.at[ct], gather_recv.at[ct, core])
+
+    @pl.when(core == 1)
+    def _():
+        wait_for(syr.reshape(2 * NY, 8, W).at[pl.ds(0, 2 * NY - 1)], lines_recv.at[0])
+        for b in (1, 0):
+            rates = columns(syr.at[b].reshape(NY * 8, W)[pl.ds(0, NY, stride=8), 0:B])
+            for ct in range(CT):
+                t, g = transfer(rates, inverse_y[:, lanes(ct)], True)
+                flat = tgy.at[b, ct].reshape(NY * 16, W)
+                for k, value in enumerate(t + g):
+                    for l in range(2):
+                        flat[pl.ds(128 * l + k, 8, stride=16), :] = value[8 * l:8 * l + 8]
+        for ct in range(CT):
+            for b in (1, 0):
+                wait_for(yr1.at[ct, b, pl.ds(0, NY - b)], gather_recv.at[ct, b])
+                chain(yr1.at[ct, b], tgy.at[b, ct], ys2.at[ct, b])
+                for offset in OFFSETS_Y:
+                    peer = peer_y(*offset)
+                    remote(ys2.at[ct, b, peer], yr2.at[ct, gy], y_sent.at[0], reply_recv.at[ct],
+                           (owner - 1 + b, peer)).start()
+                if b == 0:
+                    remote(ys2.at[ct, 0, gy], yr2.at[ct, gy], y_sent.at[0], reply_recv.at[ct], (owner - 1, gy)).start()
+                else:
+                    yr2[ct, gy] = ys2[ct, 1, gy]
 
     amplitude = 10.0 * jnp.minimum(reach, 0.25) * math.sqrt(NX * B * NY * B)
     for ct in range(CT):
-        wait_for(yr2.at[ct, pl.ds(0, NY - 1)], y_recv.at[1, ct])
+        for b in range(2):
+            pl.when(core == b)(lambda ct=ct, b=b: wait_for(yr2.at[ct, pl.ds(0, NY - b)], reply_recv.at[ct]))
         flat = yr2.at[ct].reshape(NY * 8, W)
         states = [flat[pl.ds(k, NY, stride=8), :] for k in range(8)]
 
@@ -324,17 +355,12 @@
         sweep(u.at[ct], py.at[ct], mid.at[ct], across, states[:4], states[4:], finish)
         out[:, lanes(ct)] = u[ct]
 
-    wait_for(sxr.at[0], pole_send.at[0])
-    wait_for(sxr.at[pl.ds(0, NX - 2)], pole_send.at[1])
-    wait_for(syr.at[pl.ds(0, NY - 1)], pole_send.at[2])
-    for ct in range(CT):
-        wait_for(pair.at[ct, 0], pair_send.at[ct])
-        for r in range(1, NZ):
-            pl.when(z < NZ - 1)(lambda ct=ct, r=r: start_z(ct, r, 0).wait_send())
-            pl.when(lax.rem(z + r, NZ) < z)(lambda ct=ct, r=r: start_z(ct, r, 1).wait_send())
-        wait_for(entering.at[ct, 0], back_send.at[ct])
-        wait_for(ys1.at[ct, pl.ds(0, NY - 1)], y_send.at[0, ct])
-        wait_for(ys2.at[ct, pl.ds(0, NY - 1)], y_send.at[1, ct])
+    tiles = chips.reshape(NZ * CT * 14, 8, W)
+    wait_for(tiles.at[pl.ds(0, NX - 1 + 16 * CT)], sent.at[0])
+    for chip_z, messages in enumerate((3, 4, 5, 3)):
+        pl.when(z == chip_z)(lambda messages=messages: wait_for(tiles.at[pl.ds(0, 4 * CT * messages)], z_sent.at[0]))
+    for b, messages in enumerate(((CT + 1) * NY, (CT + 1) * (NY - 1) + CT * (2 * NY - 1))):
+        pl.when(core == b)(lambda messages=messages: wait_for(tiles.at[pl.ds(0, messages)], y_sent.at[0]))
 
 
 def shards(increment, vertical, col_reach, stretch_x, stretch_y):
@@ -347,7 +373,7 @@
     def dma(*shape):
         return pltpu.SemaphoreType.DMA(shape)
 
-    two, lines = states(CT, 2, 8), states(CT, NY)
+    two, lines, both = states(CT, 2, 8), states(CT, NY), states(CT, 2, NY)
     operands = (increment.reshape(B * B, C), vertical, col_reach, stretch_x, stretch_y)
     result = pl.pallas_call(
         kernel,
@@ -360,10 +386,10 @@
             field, field, field, field,
             two, two, states(CT, 18), states(NZ, CT, 14), states(CT, NZ + 1, 4),
             states(CT, 2, 4), states(CT, NZ, 2, 4), two, two,
-            lines, lines, lines, lines, pltpu.VMEM((CT, NY, 16, W), f32),
-            states(2), states(NX), states(NY), states(NY),
-            dma(3), dma(3), dma(CT), dma(CT), dma(CT, NZ, 2), dma(CT, NZ, 2),
-            dma(CT), dma(CT), dma(2, CT), dma(2, CT),
+            lines, both, both, lines, pltpu.VMEM((2, CT, NY, 16, W), f32),
+            states(2), states(NX), states(NY), states(2, NY),
+            dma(1), dma(1), dma(1), dma(1), dma(NZ), dma(1), dma(CT),
+            dma(CT), dma(CT), dma(CT, 2), dma(CT),
         ],
         compiler_params=pltpu.CompilerParams(
             collective_id=0, has_side_effects=True, vmem_limit_bytes=32 * 2**20),

time: 27.9 us -> 26.9 us (0.964)
  Pallas kernels: 27 us -> 26 us
    pallas_call x1, Pallas kernels: 27 us -> 26 us  [shards(): pl.pallas_call(kernel, out_shape=jax.ShapeDtypeStruct((B * B, C), f32), i...]
where the time goes in v1:
time: 26.9 us; the launch traced here: 26.8 us
  Pallas kernels  26 us (97%)
  local copies, waits for them, and re-layouts  0.75 us (3%)
    pallas_call x1, Pallas kernels, shards(): pl.pallas_call(kernel, out_shape=jax.ShapeDtypeStruct((B * B, C), f32), i...  26 us
    unnamed x1, local copies, waits for them, and re-layouts  0.75 us

profile of v1, /device:TPU:1, one launch (start us, length us, event | category | flops | bytes accessed | tf_op | source)
XLA Modules:
  0.0 26.8 jit_solution(16715485445072468614)
XLA Ops:
  0.0 26.0 %covariance.1 = f32[256,384]{1,0:T(8,128)S(1)} custom-call(bf16[256,384]{1,0:T(8,128)(2,1)} %bitcast.3, bf16[384,384]{1,0:T(8,128)(2,1)} %vert_hbm.1, f32[384]{0:T(512)} %reach_hbm.1, f32[16,16]{1,0:T(8,128)} %sx_hbm.1, f32[16,16]{1,0:T(8,128)} %sy_hbm.1), custom_call_target="tpu_custom_call" | custom-call | tf_op jit(solution)/shard_map/covariance/pallas_call | solution.py:378
  26.0 0.7 %copy.7 = f32[16,16,384]{2,1,0:T(8,128)} copy(f32[16,16,384]{2,1,0:T(8,128)S(1)} %bitcast.2) | data formatting | bytes 786432

commit v2 on v1

--- a/solution.py
+++ b/solution.py
@@ -197,12 +197,12 @@
 
     pl.semaphore_wait(barrier, NX + NY - 2 + core * (NY - 1))
     remote(sxs.at[1 - core], sxr.at[gx], sent.at[0], beside_recv.at[0], other).start()
-    for ct in range(CT):
-        remote(ends_x.at[ct, 1 - core], pair.at[ct, core], sent.at[0], pair_recv.at[ct], other).start()
     for r in (2, 1, 3):
         for c in range(2):
             peer = 2 * lax.rem(z + r, NZ) + c
             remote(sxs.at[c], sxr.at[gx], sent.at[0], chip_recv.at[z], (peer, gy)).start()
+    for ct in range(CT):
+        remote(ends_x.at[ct, 1 - core], pair.at[ct, core], sent.at[0], pair_recv.at[ct], other).start()
     sxr[gx] = sxs[core]
     for ct in range(CT):
         pair[ct, core] = ends_x[ct, core]
@@ -329,8 +329,8 @@
                 for k, value in enumerate(t + g):
                     for l in range(2):
                         flat[pl.ds(128 * l + k, 8, stride=16), :] = value[8 * l:8 * l + 8]
-        for ct in range(CT):
-            for b in (1, 0):
+        for b in (1, 0):
+            for ct in range(CT):
                 wait_for(yr1.at[ct, b, pl.ds(0, NY - b)], gather_recv.at[ct, b])
                 chain(yr1.at[ct, b], tgy.at[b, ct], ys2.at[ct, b])
                 for offset in OFFSETS_Y:

time: 26.9 us -> 26.5 us (0.985)
  Pallas kernels: 26 us -> 25.5 us
    pallas_call x1, Pallas kernels: 26 us -> 25.5 us  [shards(): pl.pallas_call(kernel, out_shape=jax.ShapeDtypeStruct((B * B, C), f32), i...]
where the time goes in v2:
time: 26.5 us; the launch traced here: 26.3 us
  Pallas kernels  25.5 us (96%)
  local copies, waits for them, and re-layouts  0.75 us (3%)
    pallas_call x1, Pallas kernels, shards(): pl.pallas_call(kernel, out_shape=jax.ShapeDtypeStruct((B * B, C), f32), i...  25.5 us
    unnamed x1, local copies, waits for them, and re-layouts  0.75 us

profile of v2, /device:TPU:1, one launch (start us, length us, event | category | flops | bytes accessed | tf_op | source)
XLA Modules:
  0.0 26.3 jit_solution(12120829583037012892)
XLA Ops:
  0.0 25.5 %covariance.1 = f32[256,384]{1,0:T(8,128)S(1)} custom-call(bf16[256,384]{1,0:T(8,128)(2,1)} %bitcast.3, bf16[384,384]{1,0:T(8,128)(2,1)} %vert_hbm.1, f32[384]{0:T(512)} %reach_hbm.1, f32[16,16]{1,0:T(8,128)} %sx_hbm.1, f32[16,16]{1,0:T(8,128)} %sy_hbm.1), custom_call_target="tpu_custom_call" | custom-call | tf_op jit(solution)/shard_map/covariance/pallas_call | solution.py:378
  25.5 0.7 %copy.7 = f32[16,16,384]{2,1,0:T(8,128)} copy(f32[16,16,384]{2,1,0:T(8,128)S(1)} %bitcast.2) | data formatting | bytes 786432

commit v3 on v2

--- a/solution.py
+++ b/solution.py
@@ -14,6 +14,7 @@
 C, W, CT = 384, 128, 3
 OFFSETS_Y = sorted([(a, b) for a in range(4) for b in range(4) if a or b],
                    key=lambda o: -min(o[0], 4 - o[0]) - min(o[1], 4 - o[1]))
+ORDER = ((1, 0), (1, 1), (0, 0), (1, 2), (0, 1), (0, 2))
 PAIRS = [(a, b) for a in range(4) for b in range(a, 4)]
 
 
@@ -45,10 +46,14 @@
     return out
 
 
-def transfer(rates, scale, reflecting):
+def poles(stretch, scale):
+    return jnp.exp(-1.0 / (stretch * scale))
+
+
+def transfer(stretches, scale, reflecting):
     c, g = None, [None] * 10
-    for rate in rates:
-        p = jnp.exp(rate * scale)
+    for stretch in stretches:
+        p = poles(stretch, scale)
         q = 1.0 - p
         if c is None:
             d = [jnp.ones_like(p), q]
@@ -71,17 +76,17 @@
     return [tile[:, i:i + 1] for i in range(B)]
 
 
-def sweep(source, poles, mid, rows_of, first, second, sink=None):
+def sweep(source, pole, mid, rows_of, first, second, sink=None):
     state = first
     for i in range(B):
         rows = pl.ds(i * B, B)
-        p = poles[rows, :]
+        p = pole[rows, :]
         state, w = cascade(state, source[rows_of(i), :], p, 1.0 - p)
         mid[rows, :] = w
     ahead, state = state, second
     for i in reversed(range(B)):
         rows = pl.ds(i * B, B)
-        p = poles[rows, :]
+        p = pole[rows, :]
         state, w = cascade(state, mid[rows, :], p, 1.0 - p)
         if sink is not None:
             sink(i, w)
@@ -163,17 +168,17 @@
     loads[0].wait()
     loads[1].wait()
     reach = reach_line[...].reshape(1, C)
-    rate_x = -1.0 / sx[...].T
-    inverse_x = 1.0 / (reach * float(NX * B))
-    inverse_y = 1.0 / (reach * float(NY * B))
+    stretch_x = sx[...].T
+    scale_x = reach * float(NX * B)
+    scale_y = reach * float(NY * B)
     for i in range(B):
         for ct in range(CT):
-            px[ct, pl.ds(i * B, B), :] = jnp.exp(rate_x[:, i:i + 1] * inverse_x[:, lanes(ct)])
+            px[ct, pl.ds(i * B, B), :] = poles(stretch_x[:, i:i + 1], scale_x[:, lanes(ct)])
     loads[4].wait()
-    rate_y = -1.0 / sy[...]
+    stretch_y = sy[...]
     for half in range(2):
-        sxs[half, :, 0:B] = rate_x[8 * half:8 * half + 8]
-        sys_.reshape(NY * 8, W)[pl.ds(64 * half, 8, stride=8), 0:B] = rate_y[8 * half:8 * half + 8]
+        sxs[half, :, 0:B] = stretch_x[8 * half:8 * half + 8]
+        sys_.reshape(NY * 8, W)[pl.ds(64 * half, 8, stride=8), 0:B] = stretch_y[8 * half:8 * half + 8]
     loads[2].wait()
     loads[3].wait()
     mixed = jnp.dot(inc[...], vert[...], preferred_element_type=jnp.float32)
@@ -213,17 +218,20 @@
                       (2 * peer + core, gy))
 
     def blocks(ct):
-        t0, t1 = [own[ct, k] for k in range(4)], [own[ct, 4 + k] for k in range(4)]
-        g1 = [own[ct, 8 + n] for n in range(10)]
+        t0, t1 = [[own[ct, b, k] for k in range(4)] for b in range(2)]
+        g1 = [own[ct, 1, 4 + n] for n in range(10)]
         return t0, t1, g1, [[pair[ct, b, k] for k in range(8)] for b in range(2)]
 
+    def block_transfer(ct, b):
+        t, g = transfer(columns(sxr[2 * z + b]), scale_x[:, lanes(ct)], True)
+        for k, value in enumerate(t + g):
+            own[ct, b, k] = value
+
+    for ct in range(CT):
+        block_transfer(ct, core)
     wait_for(sxr.at[0], beside_recv.at[0])
-    first, second = columns(sxr[2 * z]), columns(sxr[2 * z + 1])
-    for ct in range(CT):
-        scale = inverse_x[:, lanes(ct)]
-        t, g = transfer(second, scale, True)
-        for k, value in enumerate(transfer(first, scale, False) + t + g):
-            own[ct, k] = value
+    for ct in range(CT):
+        block_transfer(ct, 1 - core)
         wait_for(pair.at[ct, 0], pair_recv.at[ct])
         t0, t1, g1, (e0, e1) = blocks(ct)
         ahead = toeplitz(t1, e0[:4], e1[:4])
@@ -244,20 +252,23 @@
     def left(m, _):
         rates = stretches(m)
         for ct in range(CT):
-            for k, value in enumerate(transfer(rates, inverse_x[:, lanes(ct)], False)):
+            for k, value in enumerate(transfer(rates, scale_x[:, lanes(ct)], False)):
                 chips[m, ct, k] = value
         return 0
 
     def right(m, _):
         rates = stretches(m)
         for ct in range(CT):
-            t, g = transfer(rates, inverse_x[:, lanes(ct)], True)
+            t, g = transfer(rates, scale_x[:, lanes(ct)], True)
             for k, value in enumerate(t + g):
                 chips[m, ct, k] = value
         return 0
 
     lax.fori_loop(0, z, left, 0)
     lax.fori_loop(z + 1, NZ, right, 0)
+    for i in range(B):
+        for ct in range(CT):
+            py[ct, pl.ds(i * B, B), :] = poles(stretch_y[:, i:i + 1], scale_y[:, lanes(ct)])
 
     for ct in range(CT):
         for chip_z, messages in enumerate((5, 4, 3, 3)):
@@ -299,9 +310,6 @@
         remote(back.at[ct, 1 - core], entering.at[ct, core], sent.at[0], back_recv.at[ct], other).start()
         entering[ct, core] = back[ct, core]
 
-    for i in range(B):
-        for ct in range(CT):
-            py[ct, pl.ds(i * B, B), :] = jnp.exp(rate_y[:, i:i + 1] * inverse_y[:, lanes(ct)])
 
     for ct in range(CT):
         wait_for(entering.at[ct, 0], back_recv.at[ct])
@@ -324,23 +332,22 @@
         for b in (1, 0):
             rates = columns(syr.at[b].reshape(NY * 8, W)[pl.ds(0, NY, stride=8), 0:B])
             for ct in range(CT):
-                t, g = transfer(rates, inverse_y[:, lanes(ct)], True)
+                t, g = transfer(rates, scale_y[:, lanes(ct)], True)
                 flat = tgy.at[b, ct].reshape(NY * 16, W)
                 for k, value in enumerate(t + g):
                     for l in range(2):
                         flat[pl.ds(128 * l + k, 8, stride=16), :] = value[8 * l:8 * l + 8]
-        for b in (1, 0):
-            for ct in range(CT):
-                wait_for(yr1.at[ct, b, pl.ds(0, NY - b)], gather_recv.at[ct, b])
-                chain(yr1.at[ct, b], tgy.at[b, ct], ys2.at[ct, b])
-                for offset in OFFSETS_Y:
-                    peer = peer_y(*offset)
-                    remote(ys2.at[ct, b, peer], yr2.at[ct, gy], y_sent.at[0], reply_recv.at[ct],
-                           (owner - 1 + b, peer)).start()
-                if b == 0:
-                    remote(ys2.at[ct, 0, gy], yr2.at[ct, gy], y_sent.at[0], reply_recv.at[ct], (owner - 1, gy)).start()
-                else:
-                    yr2[ct, gy] = ys2[ct, 1, gy]
+        for b, ct in ORDER:
+            wait_for(yr1.at[ct, b, pl.ds(0, NY - b)], gather_recv.at[ct, b])
+            chain(yr1.at[ct, b], tgy.at[b, ct], ys2.at[ct, b])
+            for offset in OFFSETS_Y:
+                peer = peer_y(*offset)
+                remote(ys2.at[ct, b, peer], yr2.at[ct, gy], y_sent.at[0], reply_recv.at[ct],
+                       (owner - 1 + b, peer)).start()
+            if b == 0:
+                remote(ys2.at[ct, 0, gy], yr2.at[ct, gy], y_sent.at[0], reply_recv.at[ct], (owner - 1, gy)).start()
+            else:
+                yr2[ct, gy] = ys2[ct, 1, gy]
 
     amplitude = 10.0 * jnp.minimum(reach, 0.25) * math.sqrt(NX * B * NY * B)
     for ct in range(CT):
@@ -384,7 +391,7 @@
             pltpu.VMEM((B * B, C), jnp.bfloat16), pltpu.VMEM((C, C), jnp.bfloat16), pltpu.VMEM((C,), f32),
             pltpu.VMEM((B, B), f32), pltpu.VMEM((B, B), f32), dma(5),
             field, field, field, field,
-            two, two, states(CT, 18), states(NZ, CT, 14), states(CT, NZ + 1, 4),
+            two, two, states(CT, 2, 14), states(NZ, CT, 14), states(CT, NZ + 1, 4),
             states(CT, 2, 4), states(CT, NZ, 2, 4), two, two,
             lines, both, both, lines, pltpu.VMEM((2, CT, NY, 16, W), f32),
             states(2), states(NX), states(NY), states(2, NY),

time: 26.5 us -> 26.4 us (level)
  no operation moved by 1% of the time
where the time goes in v3:
time: 26.4 us; the launch traced here: 26.3 us
  Pallas kernels  25.5 us (97%)
  local copies, waits for them, and re-layouts  0.75 us (3%)
    pallas_call x1, Pallas kernels, shards(): pl.pallas_call(kernel, out_shape=jax.ShapeDtypeStruct((B * B, C), f32), i...  25.5 us
    unnamed x1, local copies, waits for them, and re-layouts  0.75 us

profile of v3, /device:TPU:1, one launch (start us, length us, event | category | flops | bytes accessed | tf_op | source)
XLA Modules:
  0.0 26.3 jit_solution(13697459913592262120)
XLA Ops:
  0.0 25.5 %covariance.1 = f32[256,384]{1,0:T(8,128)S(1)} custom-call(bf16[256,384]{1,0:T(8,128)(2,1)} %bitcast.3, bf16[384,384]{1,0:T(8,128)(2,1)} %vert_hbm.1, f32[384]{0:T(512)} %reach_hbm.1, f32[16,16]{1,0:T(8,128)} %sx_hbm.1, f32[16,16]{1,0:T(8,128)} %sy_hbm.1), custom_call_target="tpu_custom_call" | custom-call | tf_op jit(solution)/shard_map/covariance/pallas_call | solution.py:385
  25.5 0.7 %copy.7 = f32[16,16,384]{2,1,0:T(8,128)} copy(f32[16,16,384]{2,1,0:T(8,128)S(1)} %bitcast.2) | data formatting | bytes 786432

commit v4 on v3

--- a/solution.py
+++ b/solution.py
@@ -128,8 +128,6 @@
         return lax.rem(gy // 4 + dy, 4) * 4 + lax.rem(gy + dx, 4)
 
     barrier = pltpu.get_barrier_semaphore()
-    for r in range(1, NX):
-        pl.semaphore_signal(barrier, inc=1, device_id=(lax.rem(gx + r, NX), gy), device_id_type=MESH)
     for offset in OFFSETS_Y:
         pl.semaphore_signal(barrier, inc=1, device_id=(owner, peer_y(*offset)), device_id_type=MESH)
 
@@ -137,6 +135,9 @@
     def _():
         for offset in OFFSETS_Y:
             pl.semaphore_signal(barrier, inc=1, device_id=(owner - 1, peer_y(*offset)), device_id_type=MESH)
+
+    for r in range(1, NX):
+        pl.semaphore_signal(barrier, inc=1, device_id=(lax.rem(gx + r, NX), gy), device_id_type=MESH)
 
     loads = [pltpu.make_async_copy(src, dst, load_sem.at[n]) for n, (src, dst) in enumerate(
         [(sx_hbm, sx), (reach_hbm, reach_line), (vert_hbm, vert), (inc_hbm, inc), (sy_hbm, sy)])]
@@ -207,7 +208,7 @@
             peer = 2 * lax.rem(z + r, NZ) + c
             remote(sxs.at[c], sxr.at[gx], sent.at[0], chip_recv.at[z], (peer, gy)).start()
     for ct in range(CT):
-        remote(ends_x.at[ct, 1 - core], pair.at[ct, core], sent.at[0], pair_recv.at[ct], other).start()
+        remote(ends_x.at[ct, 1 - core], pair.at[ct, core], sent.at[0], pair_recv.at[0], other).start()
     sxr[gx] = sxs[core]
     for ct in range(CT):
         pair[ct, core] = ends_x[ct, core]
@@ -232,7 +233,8 @@
     wait_for(sxr.at[0], beside_recv.at[0])
     for ct in range(CT):
         block_transfer(ct, 1 - core)
-        wait_for(pair.at[ct, 0], pair_recv.at[ct])
+        if ct == 0:
+            wait_for(chips.reshape(NZ * CT * 14, 8, W).at[pl.ds(0, 8 * CT)], pair_recv.at[0])
         t0, t1, g1, (e0, e1) = blocks(ct)
         ahead = toeplitz(t1, e0[:4], e1[:4])
         behind = toeplitz(t0, reflect(g1, e0[:4], e1[4:]), e0[4:])
@@ -395,7 +397,7 @@
             states(CT, 2, 4), states(CT, NZ, 2, 4), two, two,
             lines, both, both, lines, pltpu.VMEM((2, CT, NY, 16, W), f32),
             states(2), states(NX), states(NY), states(2, NY),
-            dma(1), dma(1), dma(1), dma(1), dma(NZ), dma(1), dma(CT),
+            dma(1), dma(1), dma(1), dma(1), dma(NZ), dma(1), dma(1),
             dma(CT), dma(CT), dma(CT, 2), dma(CT),
         ],
         compiler_params=pltpu.CompilerParams(

time: 26.4 us -> 26.4 us (level)
  no operation moved by 1% of the time
where the time goes in v4:
time: 26.4 us; the launch traced here: 26.2 us
  Pallas kernels  25.5 us (97%)
  local copies, waits for them, and re-layouts  0.75 us (3%)
    pallas_call x1, Pallas kernels, shards(): pl.pallas_call(kernel, out_shape=jax.ShapeDtypeStruct((B * B, C), f32), i...  25.5 us
    unnamed x1, local copies, waits for them, and re-layouts  0.75 us

profile of v4, /device:TPU:1, one launch (start us, length us, event | category | flops | bytes accessed | tf_op | source)
XLA Modules:
  0.0 26.2 jit_solution(11946551628279081388)
XLA Ops:
  0.0 25.5 %covariance.1 = f32[256,384]{1,0:T(8,128)S(1)} custom-call(bf16[256,384]{1,0:T(8,128)(2,1)} %bitcast.3, bf16[384,384]{1,0:T(8,128)(2,1)} %vert_hbm.1, f32[384]{0:T(512)} %reach_hbm.1, f32[16,16]{1,0:T(8,128)} %sx_hbm.1, f32[16,16]{1,0:T(8,128)} %sy_hbm.1), custom_call_target="tpu_custom_call" | custom-call | tf_op jit(solution)/shard_map/covariance/pallas_call | solution.py:387
  25.5 0.7 %copy.7 = f32[16,16,384]{2,1,0:T(8,128)} copy(f32[16,16,384]{2,1,0:T(8,128)S(1)} %bitcast.2) | data formatting | bytes 786432

commit v5 on v4

--- a/solution.py
+++ b/solution.py
@@ -272,7 +272,7 @@
         for ct in range(CT):
             py[ct, pl.ds(i * B, B), :] = poles(stretch_y[:, i:i + 1], scale_y[:, lanes(ct)])
 
-    for ct in range(CT):
+    def leave_z(ct):
         for chip_z, messages in enumerate((5, 4, 3, 3)):
             pl.when(z == chip_z)(lambda ct=ct, messages=messages: wait_for(
                 from_z.at[ct].reshape(2 * NZ, 4, 8, W).at[pl.ds(0, messages)], z_recv.at[ct]))
@@ -313,7 +313,7 @@
         entering[ct, core] = back[ct, core]
 
 
-    for ct in range(CT):
+    def enter_y(ct):
         wait_for(entering.at[ct, 0], back_recv.at[ct])
         states = [jnp.concatenate([entering[ct, half, k] for half in range(2)], axis=0) for k in range(8)]
 
@@ -327,6 +327,9 @@
             for l in range(2):
                 flat[pl.ds(64 * l + k, 8, stride=8), :] = ends[k][8 * l:8 * l + 8]
         to_owners(ys1.at[ct], yr1.at[ct], gather_recv.at[ct, core])
+
+    for stage, ct in ((leave_z, 0), (leave_z, 1), (enter_y, 0), (leave_z, 2), (enter_y, 1), (enter_y, 2)):
+        stage(ct)
 
     @pl.when(core == 1)
     def _():

time: 26.4 us -> 26.6 us (level)
  no operation moved by 1% of the time
where the time goes in v5:
time: 26.6 us; the launch traced here: 26.5 us
  Pallas kernels  25.7 us (97%)
  local copies, waits for them, and re-layouts  0.75 us (3%)
    pallas_call x1, Pallas kernels, shards(): pl.pallas_call(kernel, out_shape=jax.ShapeDtypeStruct((B * B, C), f32), i...  25.7 us
    unnamed x1, local copies, waits for them, and re-layouts  0.75 us

profile of v5, /device:TPU:1, one launch (start us, length us, event | category | flops | bytes accessed | tf_op | source)
XLA Modules:
  0.0 26.5 jit_solution(11676344225041026337)
XLA Ops:
  0.0 25.7 %covariance.1 = f32[256,384]{1,0:T(8,128)S(1)} custom-call(bf16[256,384]{1,0:T(8,128)(2,1)} %bitcast.3, bf16[384,384]{1,0:T(8,128)(2,1)} %vert_hbm.1, f32[384]{0:T(512)} %reach_hbm.1, f32[16,16]{1,0:T(8,128)} %sx_hbm.1, f32[16,16]{1,0:T(8,128)} %sy_hbm.1), custom_call_target="tpu_custom_call" | custom-call | tf_op jit(solution)/shard_map/covariance/pallas_call | solution.py:390
  25.7 0.7 %copy.7 = f32[16,16,384]{2,1,0:T(8,128)} copy(f32[16,16,384]{2,1,0:T(8,128)S(1)} %bitcast.2) | data formatting | bytes 786432
